TPU v7x, 128 devices: a whole 4x4x4 slice. The times are simulated.
128 devices in a mesh: batch: 4 (over x_lo, core), label: 32 (over z, x_hi, y).
Axes of the slice: x: 4 (x_hi: 2, x_lo: 2; x = x_hi * 2 + x_lo), y: 4, z: 4, core: 2. Of those that a mesh axis runs over, the one named last changes fastest.
Arguments:
- encoded: bfloat16 [4096, 768], P(('batch', 'label')), may hold values from -6 to 6
- label_ids: int32 [4096, 32], P(('batch', 'label')), may hold values from -1 to 131071, as said below
- weights: float32 [131072, 768], P(('batch', 'label')), may hold values from -0.21875 to 0.21875
- accum: float32 [131072, 768], P(('batch', 'label')), may hold values from 1 to 4096
Outputs:
- encoder_grad: bfloat16 [4096, 768], P(('batch', 'label'))
- new_weights: float32 [131072, 768], P(('batch', 'label'))
- new_accum: float32 [131072, 768], P(('batch', 'label'))
Inputs may be any that keep to these rules, and one draw needn't show every extreme that they name: `label_ids`: each row holds its valid ids in its first slots and -1 after them, at least one valid id; the valid ids of a row are distinct.
All inputs are finite; a program needn't handle non-finite values.
Results may differ from a plain program's by a relative error of at most 0.0098.
Values may be sent and summed in bfloat16 or wider, within the bound.
A program may use at most 128 MiB of HBM per device.

v0:
```python
import jax
import jax.numpy as jnp
from jax import lax
from jax.sharding import PartitionSpec as P


def make_delta(rows_in, ids_in, w_low, offset):
    label_rows = w_low.shape[0]
    logits = lax.dot_general(
        rows_in, w_low, (((1,), (1,)), ((), ())), preferred_element_type=jnp.float32
    )
    local = ids_in - offset
    valid = (ids_in >= 0) & (local >= 0) & (local < label_rows)
    local = jnp.where(valid, local, -1).astype(jnp.int32)
    columns = jnp.arange(label_rows, dtype=jnp.int32)[None, None, :]
    targets = jnp.any(local[:, :, None] == columns, axis=1).astype(jnp.float32)
    return (jax.nn.sigmoid(logits) - targets).astype(jnp.bfloat16)


def on_device(encoded, label_ids, weights, accum):
    label_rows = weights.shape[0]
    width = weights.shape[1]
    offset = lax.axis_index(("batch", "label")) * label_rows
    whole, ids_all = (
        lax.all_gather(encoded, ("batch", "label"), axis=0, tiled=True),
        lax.all_gather(label_ids, ("batch", "label"), axis=0, tiled=True),
    )
    w_low = weights.astype(jnp.bfloat16)
    total = whole.shape[0]
    block = min(512, total)
    count_blocks = total // block
    rows_blocked = whole.reshape(count_blocks, block, width)
    ids_blocked = ids_all.reshape(count_blocks, block, ids_all.shape[1])

    def one_block(pair):
        return make_delta(pair[0], pair[1], w_low, offset)

    delta_all = lax.map(one_block, (rows_blocked, ids_blocked)).reshape(total, label_rows)
    grad = lax.dot_general(
        delta_all, whole, (((0,), (0,)), ((), ())), preferred_element_type=jnp.float32
    )
    summed = lax.psum_scatter(
        jnp.dot(delta_all, w_low, preferred_element_type=jnp.float32),
        ("batch", "label"),
        scatter_dimension=0,
        tiled=True,
    )
    new_accum = accum + grad * grad
    new_weights = weights - 0.5 * grad / jnp.sqrt(new_accum)
    return (summed.astype(jnp.bfloat16), new_weights, new_accum)


def solution(mesh):
    return jax.shard_map(
        on_device,
        mesh=mesh,
        in_specs=(
            P(("batch", "label"), None),
            P(("batch", "label"), None),
            P(("batch", "label"), None),
            P(("batch", "label"), None),
        ),
        out_specs=(
            P(("batch", "label"), None),
            P(("batch", "label"), None),
            P(("batch", "label"), None),
        ),
        check_vma=False,
    )
```

profile of v0, /device:TPU:0, one launch (start us, length us, event | category | flops | bytes accessed | tf_op | source)
XLA Modules:
  0.0 1150.1 jit_solution(12050575668254136568)
XLA Ops:
  7.2 0.0 copy-start.1
  7.2 0.0 all-gather.2.cloned.1.call-start
  7.2 0.7 all-gather.2.cloned.1.call-update
  7.9 0.0 reduce-scatter.2.cloned.1.call-start
  8.0 3.2 convert_element_type.12
  11.2 0.0 copy-done.1
  11.2 332.3 %all_gather.7 = s32[4096,32]{1,0:T(8,128)S(1)} all-gather(s32[32,32]{1,0:T(8,128)S(1)} %copy-done.1), channel_id=1, replica_groups=mesh['batch'=4,'label'=32] {'batch','label'}, dimensions={0}, use_global_device_ids=true | all-gather | bytes 528384 | tf_op jit(solution)/shard_map/all_gather | solution.py:26
  343.5 0.0 all-gather.2.cloned.1.call-done
  343.5 106.1 %while.10 = (s32[]{:T(128)}, bf16[8,512,1024]{2,1,0:T(8,128)(2,1)}, bf16[8,512,768]{2,1,0:T(8,128)(2,1)}, bf16[1024,768]{1,0:T(8,128)(2,1)}, s32[8,512,32]{2,1,0:T(8,128)S(1)}, /*index=5*/s32[]{:T(128)}, s32[]{:T(128)}) while((s32[]{:T(128)}, bf16[8,512,1024]{2,1,0:T(8,128)(2,1)}, bf16[8,512,768]{2,1,0:T(8,128)(2,1)}, ...), condition=%wide.region_2.3_spmd, body=%wide.region_0.2_spmd.sunk | while | flops 841596928 | bytes 4654173 | solution.py:38
  343.5 0.1 bitcast_select_fusion.2
  343.6 9.3 fusion.20
  352.8 4.0 fusion.21
  356.8 0.1 bitcast_select_fusion.2
  356.9 9.3 fusion.20
  366.1 3.9 fusion.21
  370.0 0.1 bitcast_select_fusion.2
  370.1 9.3 fusion.20
  379.4 3.9 fusion.21
  383.3 0.1 bitcast_select_fusion.2
  383.4 9.3 fusion.20
  392.6 3.9 fusion.21
  396.5 0.1 bitcast_select_fusion.2
  396.6 9.3 fusion.20
  405.9 3.9 fusion.21
  409.8 0.1 bitcast_select_fusion.2
  409.8 9.3 fusion.20
  419.1 3.9 fusion.21
  423.0 0.1 bitcast_select_fusion.2
  423.1 9.3 fusion.20
  432.4 3.9 fusion.21
  436.3 0.1 bitcast_select_fusion.2
  436.4 9.3 fusion.20
  445.6 3.9 fusion.21
  449.6 12.2 %fusion.8 = f32[4096,768]{1,0:T(8,128)} fusion(bf16[4096,1024]{1,0:T(8,128)(2,1)} %bitcast.39, bf16[1024,768]{1,0:T(8,128)(2,1)} %get-tuple-element.114), kind=kOutput, calls=%fused_computation.15 | convolution fusion | flops 6442450944 | bytes 22544384 | tf_op jit(solution)/shard_map/dot_general | solution.py:43
  461.8 0.0 copy-start
  461.8 0.0 reduce-scatter.2.cloned.1.call-update
  461.8 1.9 copy-done
  463.7 13.4 %multiply_subtract_fusion = (f32[1024,768]{1,0:T(8,128)}, f32[1024,768]{1,0:T(8,128)}) fusion(f32[1024,768]{1,0:T(8,128)S(1)} %copy-done, f32[1024,768]{1,0:T(8,128)} %param.9, bf16[4096,1024]{1,0:T(8,128)(2,1)} %bitcast.40, bf16[4096,768]{1,0:T(8,128)(2,1)} %bitcast.42), kind=kOutput, calls=%fused_computation.13 | convolution fusion | flops 6446383104 | bytes 27262976 | tf_op jit(solution)/shard_map/dot_general | solution.py:39
  477.0 664.8 %reduce-scatter.2.cloned.1.call-done = f32[32,768]{1,0:T(8,128)} async-done(((f32[4096,768]{1,0:T(8,128)}), f32[32,768]{1,0:T(8,128)}) %reduce-scatter.2.cloned.1.call-update) | async-done | bytes 98320 | tf_op jit(solution)/shard_map/reduce_scatter | solution.py:42
  1141.8 1.5 convert_element_type.13
  (1 shorter events, 0.0 us)
Async XLA Ops:
  7.2 4.0 copy-start.1
  7.2 336.3 %all-gather.2.cloned.1.call-start = ((), (), s32[]{:S(2)}) async-start(), calls=%async_computation.1 | async-start | bytes 6340608 | tf_op jit(solution)/shard_map/all_gather | solution.py:25
  7.9 1133.9 %reduce-scatter.2.cloned.1.call-start = ((), (), s32[]{:S(2)}) async-start(), calls=%async_computation.2 | async-start | bytes 12681216 | tf_op jit(solution)/shard_map/reduce_scatter | solution.py:42
  461.8 1.9 copy-start
Sparse Core Ops, SparseCore 0:
  9.7 313.3 all-gather.1
  461.9 679.8 reduce-scatter.1
where the time goes:
time: 1150 us
  waiting for transfers between devices  665 us (58%)
  blocking collectives  332 us (29%)
  other arithmetic  79.4 us (7%)
  matrix products  56.9 us (5%)
  between operations  14.1 us (1%)
    reduce_scatter x1, waiting for transfers between devices, on_device(): lax.psum_scatter(jnp.dot(delta_all, w_low, preferred_element_type=jnp.flo...  665 us
    all_gather x1, blocking collectives, on_device(): lax.all_gather(label_ids, ('batch', 'label'), axis=0, tiled=True)  332 us
    reduce_or x8, other arithmetic, make_delta(): targets = jnp.any(local[:, :, None] == columns, axis=1).astype(jnp.float32)  74.2 us
    dot_general x8, matrix products, make_delta(): lax.dot_general(rows_in, w_low, (((1,), (1,)), ((), ())), preferred_eleme...  31.3 us
  transfers between devices with their start and end apart: 2, of which 1 were waited for; matrix products, arithmetic and copies ran while one was open for 1% of the time, Pallas kernels for 0%

commit v1 on v0

v1 whole, which is shorter than its diff:
```python
import functools

import jax
import jax.numpy as jnp
from jax import lax
from jax.experimental import pallas as pl
from jax.experimental.pallas import tpu as pltpu
from jax.sharding import PartitionSpec as P

MESH = pl.DeviceIdType.MESH
NT = (((1,), (1,)), ((), ()))
TN = (((0,), (0,)), ((), ()))
GATHER_ORDER = ((0, 1, 2), (1, 2, 0), (2, 0, 1), (0, 1, 2))
SCATTER_ORDER = ((0, 1, 2), (1, 2, 0), (2, 0, 1))
F32 = jnp.float32
BF16 = jnp.bfloat16


def place(n):
    batch, label = lax.axis_index("batch"), lax.axis_index("label")
    core = lax.rem(batch, 2)
    x = lax.rem(lax.div(label, n), n // 2) * 2 + lax.div(batch, 2)
    y = lax.rem(label, n)
    z = lax.div(label, n * (n // 2))
    return (x, y, z), core


def device(n, xyz, core):
    x, y, z = xyz
    return (
        lax.rem(x, 2) * 2 + core,
        z * (n * (n // 2)) + lax.div(x, 2) * n + y,
    )


def kernel(
    n, enc_ref, ids_ref, w_ref, out_ref, grad_ref,
    rows, ids, w_wide, w_low, mask, delta, part, from_core, recv1, sum2, recv2, sum3, recv3, pad,
    w_sem, g_send, g_recv, c_send, c_recv, x_send, x_recv, s_send, s_recv,
):
    me, core = place(n)
    other = 1 - core
    labels = w_ref.shape[0]
    batch, label = lax.axis_index("batch"), lax.axis_index("label")
    offset = (batch * lax.axis_size("label") + label) * labels
    sibling = device(n, me, other)

    def shifted(axis, by):
        return tuple(lax.rem(me[a] + by, n) if a == axis else me[a] for a in range(3))

    w_copy = pltpu.make_async_copy(w_ref, w_wide, w_sem)
    w_copy.start()

    barrier = pltpu.get_barrier_semaphore()
    for axis in range(3):
        for by in range(1, n):
            pl.semaphore_signal(
                barrier, inc=1, device_id=device(n, shifted(axis, by), core), device_id_type=MESH
            )
    pl.semaphore_signal(barrier, inc=1, device_id=sibling, device_id_type=MESH)

    for j in range(3):
        rows[(j, core) + me] = enc_ref[:, j * 256 : (j + 1) * 256]
    pad[:, 0:32] = ids_ref[...]
    lane8 = lax.broadcasted_iota(jnp.int32, (8, 128), 1)
    turned = jnp.concatenate([pad[...]] * 4, axis=0).T
    packed = turned[0:8]
    for q in range(1, 4):
        packed = jnp.where(lax.shift_right_logical(lane8, 5) == q, turned[8 * q : 8 * q + 8], packed)
    ids[(core,) + me] = packed

    pl.semaphore_wait(barrier, 3 * (n - 1) + 1)

    def gathered(j, index):
        return rows.at[(j, core) + index] if j < 3 else ids.at[(core,) + index]

    def g_copy(j, step, by):
        order = GATHER_ORDER[j]
        index = tuple(slice(None) if a in order[:step] else me[a] for a in range(3))
        ref = gathered(j, index)
        return pltpu.make_async_remote_copy(
            src_ref=ref, dst_ref=ref,
            send_sem=g_send.at[j, step, by - 1], recv_sem=g_recv.at[j, step, by - 1],
            device_id=device(n, shifted(order[step], by), core), device_id_type=MESH,
        )

    def c_copy(j, by):
        last = GATHER_ORDER[j][2]
        plane = lax.rem(me[last] + n - by, n)
        ref = gathered(j, tuple(plane if a == last else slice(None) for a in range(3)))
        return pltpu.make_async_remote_copy(
            src_ref=ref, dst_ref=ref, send_sem=c_send.at[j, by], recv_sem=c_recv.at[j, by],
            device_id=sibling, device_id_type=MESH,
        )

    pieces = (3, 0, 1, 2)
    for step in range(3):
        for j in pieces:
            if step > 0:
                for by in range(1, n):
                    g_copy(j, step - 1, by).wait_recv()
            for by in range(1, n):
                g_copy(j, step, by).start()
            if step == 2:
                c_copy(j, 0).start()

    w_copy.wait()

    def narrow(i, _):
        at = pl.ds(pl.multiple_of(i * 128, 128), 128)
        for j in range(3):
            w_low[j, at, :] = w_wide[at, j * 256 : (j + 1) * 256].astype(BF16)
        return 0

    lax.fori_loop(0, labels // 128, narrow, 0)

    for by in range(1, n):
        for j in pieces:
            g_copy(j, 2, by).wait_recv()
            c_copy(j, by).start()
    for by in range(n):
        for j in pieces:
            c_copy(j, by).wait_recv()

    sub8 = lax.broadcasted_iota(jnp.int32, (8, 128), 0)
    lane_all = lax.broadcasted_iota(jnp.int32, (128, 128), 1)

    def mask_block(cx, _):
        four = ids[lax.div(cx, n), lax.rem(cx, n)].reshape(n * n, 8, 128)
        for g in range(n * n // 4):
            total = [None] * 4
            for q in range(4):
                local = four[4 * g + q] - offset
                valid = (local >= 0) & (local < labels)
                word = jnp.where(valid, local & 31, -1)
                bit = jnp.left_shift(jnp.int32(1), lax.shift_right_arithmetic(local, 5) & 31)
                held = [None] * 4
                for r in range(8):
                    word_r = jnp.broadcast_to(word[r : r + 1], (8, 128))
                    bit_r = jnp.broadcast_to(bit[r : r + 1], (8, 128))
                    for v in range(4):
                        hit = jnp.where(word_r == sub8 + 8 * v, bit_r, 0)
                        held[v] = hit if held[v] is None else held[v] | hit
                for v in range(4):
                    a = held[v] | pltpu.roll(held[v], 32, 1)
                    a = a | pltpu.roll(a, 64, 1)
                    total[v] = a if q == 0 else jnp.where(lax.shift_right_logical(lane8, 5) == q, a, total[v])
            bits = jnp.concatenate(total * 4, axis=0).T
            bits = lax.shift_right_logical(bits, lax.shift_right_logical(lane_all, 5))
            mask[cx, 4 * g : 4 * g + 4] = bits.reshape(4, 32, 128)
        return 0

    lax.fori_loop(0, 2 * n, mask_block, 0)

    tile = n * n * 16

    def half(h):
        return slice(16 * h, 16 * h + 16)

    def forward(h, c):
        def one(x, _):
            logits = None
            for j in range(3):
                e = rows[j, c, x, :, :, half(h), :].reshape(tile, 256)
                term = lax.dot_general(e, w_low[j], NT, preferred_element_type=F32)
                logits = term if logits is None else logits + term
            bits = mask[c * n + x, :, half(h), :].reshape(tile, 128)
            for t in range(labels // 128):
                sign = jnp.where((bits & (1 << (4 * t))) != 0, -1.0, 1.0)
                at = slice(128 * t, 128 * t + 128)
                delta[h, c, x, :, at] = (jnp.tanh(0.5 * logits[:, at]) + sign).astype(BF16)
            return 0

        lax.fori_loop(0, n, one, 0)

    def encoder_part(h, c, j):
        d = delta[h, c].reshape(n * tile, labels)
        r = jnp.dot(d, w_low[j], preferred_element_type=F32)
        part[j, h, c] = (0.5 * r).astype(BF16).reshape(n, n, n, 16, 256)

    def x_copy(j, h):
        return pltpu.make_async_remote_copy(
            src_ref=part.at[j, h, other], dst_ref=from_core.at[j, h],
            send_sem=x_send.at[j, h], recv_sem=x_recv.at[j, h],
            device_id=sibling, device_id_type=MESH,
        )

    def s_copy(j, h, step, by):
        order = SCATTER_ORDER[j]
        left = [a for a in range(3) if a not in order[:step]]
        to = shifted(order[step], by)
        index = tuple(to[a] if a == order[step] else slice(None) for a in left)
        src = (part.at[(j, h, core) + index], sum2.at[(j, h) + index], sum3.at[(j, h) + index])[step]
        dst = (recv1, recv2, recv3)[step].at[j, h, by - 1]
        return pltpu.make_async_remote_copy(
            src_ref=src, dst_ref=dst,
            send_sem=s_send.at[step, j, h, by - 1], recv_sem=s_recv.at[step, j, h, by - 1],
            device_id=device(n, to, core), device_id_type=MESH,
        )

    def own(j, h, step):
        order = SCATTER_ORDER[j]
        left = [a for a in range(3) if a not in order[:step]]
        index = tuple(me[a] if a == order[step] else slice(None) for a in left)
        ref = (part, sum2, sum3)[step]
        return ref[((j, h, core) if step == 0 else (j, h)) + index].astype(F32)

    def send(j, h, step):
        for by in range(1, n):
            s_copy(j, h, step, by).start()

    def add_core(h):
        for j in range(3):
            x_copy(j, h).wait_recv()

            def one(x, _):
                total = part[j, h, core, x].astype(F32) + from_core[j, h, x].astype(F32)
                part[j, h, core, x] = total.astype(BF16)
                return 0

            lax.fori_loop(0, n, one, 0)
            send(j, h, 0)

    def reduce(h, step):
        for j in range(3):
            for by in range(1, n):
                s_copy(j, h, step, by).wait_recv()
            total = own(j, h, step)
            for by in range(1, n):
                total = total + (recv1, recv2, recv3)[step][j, h, by - 1].astype(F32)
            if step == 2:
                out_ref[half(h), j * 256 : (j + 1) * 256] = total.astype(BF16)
            else:
                (sum2, sum3)[step][j, h] = total.astype(BF16)
                send(j, h, step + 1)

    def grad_part(t, j):
        at = slice(t * (labels // 2), (t + 1) * (labels // 2))
        total = None
        for h in range(2):
            for c in range(2):
                d = delta[h, c, :, :, at].reshape(n * tile, labels // 2)
                e = rows[j, c, :, :, :, half(h), :].reshape(n * tile, 256)
                term = lax.dot_general(d, e, TN, preferred_element_type=F32)
                total = term if total is None else total + term
        grad_ref[at, j * 256 : (j + 1) * 256] = 0.5 * total

    def block(h, c, send_it):
        forward(h, c)
        for j in range(3):
            encoder_part(h, c, j)
            if send_it:
                x_copy(j, h).start()

    block(0, other, True)
    block(0, core, False)
    add_core(0)
    block(1, other, True)
    reduce(0, 0)
    block(1, core, False)
    add_core(1)
    reduce(0, 1)
    grad_part(0, 0)
    grad_part(0, 1)
    reduce(0, 2)
    grad_part(0, 2)
    reduce(1, 0)
    grad_part(1, 0)
    reduce(1, 1)
    grad_part(1, 1)
    reduce(1, 2)
    grad_part(1, 2)

    for j in range(4):
        for step in range(3):
            for by in range(1, n):
                g_copy(j, step, by).wait_send()
        for by in range(n):
            c_copy(j, by).wait_send()
    for j in range(3):
        for h in range(2):
            x_copy(j, h).wait_send()
            for step in range(3):
                for by in range(1, n):
                    s_copy(j, h, step, by).wait_send()


def gradients(n, encoded, label_ids, weights):
    labels, width = weights.shape
    vmem = pltpu.VMEM
    dma = pltpu.SemaphoreType.DMA
    return pl.pallas_call(
        functools.partial(kernel, n),
        out_shape=(
            jax.ShapeDtypeStruct(encoded.shape, BF16),
            jax.ShapeDtypeStruct((labels, width), F32),
        ),
        in_specs=[
            pl.BlockSpec(memory_space=pltpu.VMEM),
            pl.BlockSpec(memory_space=pltpu.VMEM),
            pl.BlockSpec(memory_space=pl.ANY),
        ],
        out_specs=(
            pl.BlockSpec(memory_space=pltpu.VMEM),
            pl.BlockSpec(memory_space=pltpu.VMEM),
        ),
        scratch_shapes=[
            vmem((3, 2, n, n, n, 32, 256), BF16),
            vmem((2, n, n, n, 8, 128), jnp.int32),
            vmem((labels, width), F32),
            vmem((3, labels, 256), BF16),
            vmem((2 * n, n * n, 32, 128), jnp.int32),
            vmem((2, 2, n, n * n * 16, labels), BF16),
            vmem((3, 2, 2, n, n, n, 16, 256), BF16),
            vmem((3, 2, n, n, n, 16, 256), BF16),
            vmem((3, 2, n - 1, n, n, 16, 256), BF16),
            vmem((3, 2, n, n, 16, 256), BF16),
            vmem((3, 2, n - 1, n, 16, 256), BF16),
            vmem((3, 2, n, 16, 256), BF16),
            vmem((3, 2, n - 1, 16, 256), BF16),
            vmem((32, 128), jnp.int32),
            dma,
            dma((4, 3, n - 1)),
            dma((4, 3, n - 1)),
            dma((4, n)),
            dma((4, n)),
            dma((3, 2)),
            dma((3, 2)),
            dma((3, 3, 2, n - 1)),
            dma((3, 3, 2, n - 1)),
        ],
        compiler_params=pltpu.CompilerParams(
            collective_id=0, has_side_effects=True, vmem_limit_bytes=60 * 2**20
        ),
    )(encoded, label_ids, weights)


def on_device(n, encoded, label_ids, weights, accum):
    encoder_grad, grad = gradients(n, encoded, label_ids, weights)
    new_accum = accum + grad * grad
    new_weights = weights - 0.5 * grad / jnp.sqrt(new_accum)
    return (encoder_grad, new_weights, new_accum)


def solution(mesh):
    n = {4: 2, 32: 4}[mesh.shape["label"]]
    rows = P(("batch", "label"), None)
    return jax.shard_map(
        functools.partial(on_device, n),
        mesh=mesh,
        in_specs=(rows, rows, rows, rows),
        out_specs=(rows, rows, rows),
        check_vma=False,
    )
```

time: 1150 us -> 93.6 us (0.08)
  waiting for transfers between devices: 665 us -> 0 us
  blocking collectives: 332 us -> 0 us
  Pallas kernels: 0 us -> 86.1 us
  other arithmetic: 79.4 us -> 6.17 us
  matrix products: 56.9 us -> 0 us
  between operations: 14.1 us -> 0.66 us
    reduce_scatter x1 -> x0, waiting for transfers between devices: 665 us -> none  [on_device(): lax.psum_scatter(jnp.dot(delta_all, w_low, preferred_element_type=jnp.flo...]
    all_gather x1 -> x0, blocking collectives: 332 us -> none  [on_device(): lax.all_gather(label_ids, ('batch', 'label'), axis=0, tiled=True)]
    pallas_call x0 -> x1, Pallas kernels: none -> 86.1 us  [gradients(): pl.pallas_call(functools.partial(kernel, n), out_shape=(jax.ShapeDtypeStr...]
    reduce_or x8 -> x0, other arithmetic: 74.2 us -> none  [make_delta(): targets = jnp.any(local[:, :, None] == columns, axis=1).astype(jnp.float32)]
    dot_general x10 -> x0, matrix products: 56.9 us -> none  [the longest x8 31.3 us: make_delta(): lax.dot_general(rows_in, w_low, (((1,), (1,)), ((), ())), preferred_eleme...]
  transfers between devices with their start and end apart: 2 -> 0, of which waited for: 1 -> 0; matrix products, arithmetic and copies ran while one was open for 1% -> 0% of each run, Pallas kernels for 0% -> 0%
where the time goes in v1:
time: 93.6 us; the launch traced here: 93.5 us
  Pallas kernels  86.1 us (92%)
  other arithmetic  6.17 us (7%)
    pallas_call x1, Pallas kernels, gradients(): pl.pallas_call(functools.partial(kernel, n), out_shape=(jax.ShapeDtypeStr...  86.1 us
    sub x1, other arithmetic, on_device(): new_weights = weights - 0.5 * grad / jnp.sqrt(new_accum)  6.17 us

profile of v1, /device:TPU:0, one launch (start us, length us, event | category | flops | bytes accessed | tf_op | source)
XLA Modules:
  0.0 93.5 jit_solution(6987542964211147288)
XLA Ops:
  0.6 0.0 copy-start
  0.6 86.1 %shard_map.67 = (bf16[32,768]{1,0:T(8,128)(2,1)}, f32[1024,768]{1,0:T(8,128)}) custom-call(bf16[32,768]{1,0:T(8,128)(2,1)} %enc_ref.1, s32[32,32]{1,0:T(8,128)} %ids_ref.1, f32[1024,768]{1,0:T(8,128)} %w_ref.1), custom_call_target="tpu_custom_call" | custom-call | tf_op jit(solution)/shard_map/pallas_call | solution.py:292
  86.7 0.0 copy-done
  86.7 0.0 copy-start.1
  86.7 6.2 %multiply_subtract_fusion = (f32[1024,768]{1,0:T(8,128)}, f32[1024,768]{1,0:T(8,128)}) fusion(f32[1024,768]{1,0:T(8,128)S(1)} %copy-done, f32[1024,768]{1,0:T(8,128)} %get-tuple-element.6, f32[1024,768]{1,0:T(8,128)} %param.7), kind=kLoop, calls=%fused_computation | loop fusion | flops 3932160 | bytes 15728640 | tf_op jit(solution)/shard_map/sub | solution.py:341
  92.9 0.0 copy-done.1
  92.9 0.6 copy.8
Async XLA Ops:
  0.6 86.1 %copy-start = (f32[1024,768]{1,0:T(8,128)S(1)}, f32[1024,768]{1,0:T(8,128)}, u32[]{:S(2)}) copy-start(f32[1024,768]{1,0:T(8,128)} %w_ref.1) | copy-start | bytes 9437188
  86.7 6.2 %copy-start.1 = (bf16[32,768]{1,0:T(8,128)(2,1)S(1)}, bf16[32,768]{1,0:T(8,128)(2,1)}, u32[]{:S(2)}) copy-start(bf16[32,768]{1,0:T(8,128)(2,1)} %get-tuple-element.12) | copy-start | bytes 147460

commit v2 on v1

--- a/solution.py
+++ b/solution.py
@@ -35,8 +35,8 @@
 
 def kernel(
     n, enc_ref, ids_ref, w_ref, out_ref, grad_ref,
-    rows, ids, w_wide, w_low, mask, delta, part, from_core, recv1, sum2, recv2, sum3, recv3, pad,
-    w_sem, g_send, g_recv, c_send, c_recv, x_send, x_recv, s_send, s_recv,
+    rows, ids, w_wide, w_low, mask, delta, part, from_core, recv1, sum2, recv2, sum3, recv3, pad, grad,
+    w_sem, grad_sem, g_sent_all, g_sent_half, id_sent, g_recv, c_sent, c_recv, x_sent, x_recv, s_sent, s_recv,
 ):
     me, core = place(n)
     other = 1 - core
@@ -71,38 +71,99 @@
 
     pl.semaphore_wait(barrier, 3 * (n - 1) + 1)
 
+    def half(h):
+        return slice(16 * h, 16 * h + 16)
+
     def gathered(j, index):
         return rows.at[(j, core) + index] if j < 3 else ids.at[(core,) + index]
 
-    def g_copy(j, step, by):
+    def remote(src, dst, send_sem, recv_sem, to):
+        return pltpu.make_async_remote_copy(
+            src_ref=src, dst_ref=dst, send_sem=send_sem, recv_sem=recv_sem,
+            device_id=to, device_id_type=MESH,
+        )
+
+    def wait_for(ref, sem):
+        pltpu.make_async_copy(ref, ref, sem).wait()
+
+    def block_of(j, index, h):
+        return gathered(j, index + (half(h),) if j < 3 else index)
+
+    def g_sent(j, step):
+        return (id_sent if j == 3 else g_sent_all).at[step]
+
+    def g_copy(j, step, by, h=0, sem=None):
         order = GATHER_ORDER[j]
         index = tuple(slice(None) if a in order[:step] else me[a] for a in range(3))
-        ref = gathered(j, index)
-        return pltpu.make_async_remote_copy(
-            src_ref=ref, dst_ref=ref,
-            send_sem=g_send.at[j, step, by - 1], recv_sem=g_recv.at[j, step, by - 1],
-            device_id=device(n, shifted(order[step], by), core), device_id_type=MESH,
+        ref = block_of(j, index, h)
+        to = device(n, shifted(order[step], by), core)
+        return remote(ref, ref, g_sent(j, step), g_recv.at[j, h, step if sem is None else sem], to)
+
+    def g_wait(j, step, h=0):
+        order = GATHER_ORDER[j]
+        index = tuple(
+            slice(None) if a in order[:step] else slice(0, n - 1) if a == order[step] else 0 for a in range(3)
         )
-
-    def c_copy(j, by):
-        last = GATHER_ORDER[j][2]
-        plane = lax.rem(me[last] + n - by, n)
-        ref = gathered(j, tuple(plane if a == last else slice(None) for a in range(3)))
-        return pltpu.make_async_remote_copy(
-            src_ref=ref, dst_ref=ref, send_sem=c_send.at[j, by], recv_sem=c_recv.at[j, by],
-            device_id=sibling, device_id_type=MESH,
-        )
-
-    pieces = (3, 0, 1, 2)
-    for step in range(3):
-        for j in pieces:
-            if step > 0:
+        wait_for(block_of(j, index, h), g_recv.at[j, h, step])
+
+    def g_start(j, step, h=0):
+        if step > 0:
+            g_wait(j, step - 1, h)
+        if step == 2:
+            c_copy(j, 0, h).start()
+        if step == 2 and j < 3 and n == 4:
+            g_copy(j, 2, 1, h, 2).start()
+            g_copy(j, 2, 3, h, 3).start()
+        else:
+            for by in range(1, n):
+                g_copy(j, step, by, h).start()
+
+    def plane(j, by, h, at=slice(None)):
+        first, _, last = GATHER_ORDER[j]
+        to = lax.rem(me[last] + n - by, n)
+        return block_of(j, tuple(to if a == last else at if a == first else slice(None) for a in range(3)), h)
+
+    def c_copy(j, by, h=0):
+        ref = plane(j, by, h)
+        return remote(ref, ref, c_sent.at[j // 3], c_recv.at[j, h], sibling)
+
+    def hand_on(h):
+        if n == 4:
+            for by, at in ((1, slice(0, n // 2)), (3, slice(n // 2, n))):
+                for j in thirds:
+                    wait_for(plane(j, by, h), g_recv.at[j, h, 2 if by == 1 else 3])
+                    ref = plane(j, by, h, at)
+                    last = GATHER_ORDER[j][2]
+                    remote(ref, ref, g_sent_half, g_recv.at[j, h, 4], device(n, shifted(last, by), core)).start()
+                    c_copy(j, by, h).start()
+
+    def pass_on(h):
+        for j in thirds:
+            if n == 4:
+                wait_for(plane(j, 2, h), g_recv.at[j, h, 4])
+                c_copy(j, 2, h).start()
+            else:
+                g_wait(j, 2, h)
                 for by in range(1, n):
-                    g_copy(j, step - 1, by).wait_recv()
-            for by in range(1, n):
-                g_copy(j, step, by).start()
-            if step == 2:
-                c_copy(j, 0).start()
+                    c_copy(j, by, h).start()
+
+    def pass_on_ids():
+        g_wait(3, 2)
+        for by in range(1, n):
+            c_copy(3, by).start()
+
+    def await_core(js, h=0):
+        for j in js:
+            wait_for(block_of(j, (slice(None),) * 3, h), c_recv.at[j, h])
+
+    thirds = (0, 1, 2)
+    for j, step, h in (
+        (3, 0, 0), (0, 0, 0), (1, 0, 0), (2, 0, 0),
+        (3, 1, 0), (0, 1, 0), (1, 1, 0), (2, 1, 0),
+        (3, 2, 0), (0, 0, 1), (1, 0, 1), (2, 0, 1),
+        (0, 2, 0), (1, 2, 0), (2, 2, 0),
+    ):
+        g_start(j, step, h)
 
     w_copy.wait()
 
@@ -113,14 +174,6 @@
         return 0
 
     lax.fori_loop(0, labels // 128, narrow, 0)
-
-    for by in range(1, n):
-        for j in pieces:
-            g_copy(j, 2, by).wait_recv()
-            c_copy(j, by).start()
-    for by in range(n):
-        for j in pieces:
-            c_copy(j, by).wait_recv()
 
     sub8 = lax.broadcasted_iota(jnp.int32, (8, 128), 0)
     lane_all = lax.broadcasted_iota(jnp.int32, (128, 128), 1)
@@ -150,12 +203,10 @@
             mask[cx, 4 * g : 4 * g + 4] = bits.reshape(4, 32, 128)
         return 0
 
-    lax.fori_loop(0, 2 * n, mask_block, 0)
+    def make_mask(c):
+        lax.fori_loop(c * n, c * n + n, mask_block, 0)
 
     tile = n * n * 16
-
-    def half(h):
-        return slice(16 * h, 16 * h + 16)
 
     def forward(h, c):
         def one(x, _):
@@ -168,22 +219,46 @@
             for t in range(labels // 128):
                 sign = jnp.where((bits & (1 << (4 * t))) != 0, -1.0, 1.0)
                 at = slice(128 * t, 128 * t + 128)
-                delta[h, c, x, :, at] = (jnp.tanh(0.5 * logits[:, at]) + sign).astype(BF16)
+                d = (jnp.tanh(0.5 * logits[:, at]) + sign).astype(BF16)
+                delta[h, c, x, :, :, :, at] = d.reshape(n, n, 16, 128)
             return 0
 
-        lax.fori_loop(0, n, one, 0)
+        lax.fori_loop(0, n, one, 0, unroll=True)
 
     def encoder_part(h, c, j):
-        d = delta[h, c].reshape(n * tile, labels)
-        r = jnp.dot(d, w_low[j], preferred_element_type=F32)
+        r = jnp.dot(delta[h, c].reshape(n * tile, labels), w_low[j], preferred_element_type=F32)
         part[j, h, c] = (0.5 * r).astype(BF16).reshape(n, n, n, 16, 256)
 
+    def encoder_quarter(h, j, place):
+        at = tuple(place if a == j else slice(None) for a in range(3))
+        d = delta[(h, core) + at].reshape(tile, labels)
+        r = 0.5 * jnp.dot(d, w_low[j], preferred_element_type=F32)
+        r = r + from_core[(j, h) + at].reshape(tile, 256).astype(F32)
+        part[(j, h, core) + at] = r.astype(BF16).reshape(n, n, 16, 256)
+
+    def for_sibling(h):
+        encoder_part(h, other, 0)
+        encoder_part(h, other, 1)
+        x_copy(0, h).start()
+        x_copy(1, h).start()
+        encoder_part(h, other, 2)
+        x_copy(2, h).start()
+
+    def for_self(h):
+        for j in thirds:
+            wait_for(from_core.at[j, h], x_recv.at[j, h])
+        far = (2, 1, 3, 0) if n == 4 else tuple(range(n - 1, -1, -1))
+        for some in (far[: n // 2], far[n // 2 :]):
+            for by in some:
+                for j in thirds:
+                    encoder_quarter(h, j, lax.rem(me[j] + by, n))
+            for by in some:
+                for j in thirds:
+                    if by > 0:
+                        s_copy(j, h, 0, by).start()
+
     def x_copy(j, h):
-        return pltpu.make_async_remote_copy(
-            src_ref=part.at[j, h, other], dst_ref=from_core.at[j, h],
-            send_sem=x_send.at[j, h], recv_sem=x_recv.at[j, h],
-            device_id=sibling, device_id_type=MESH,
-        )
+        return remote(part.at[j, h, other], from_core.at[j, h], x_sent, x_recv.at[j, h], sibling)
 
     def s_copy(j, h, step, by):
         order = SCATTER_ORDER[j]
@@ -192,11 +267,7 @@
         index = tuple(to[a] if a == order[step] else slice(None) for a in left)
         src = (part.at[(j, h, core) + index], sum2.at[(j, h) + index], sum3.at[(j, h) + index])[step]
         dst = (recv1, recv2, recv3)[step].at[j, h, by - 1]
-        return pltpu.make_async_remote_copy(
-            src_ref=src, dst_ref=dst,
-            send_sem=s_send.at[step, j, h, by - 1], recv_sem=s_recv.at[step, j, h, by - 1],
-            device_id=device(n, to, core), device_id_type=MESH,
-        )
+        return remote(src, dst, s_sent.at[step], s_recv.at[step, j, h], device(n, to, core))
 
     def own(j, h, step):
         order = SCATTER_ORDER[j]
@@ -209,22 +280,9 @@
         for by in range(1, n):
             s_copy(j, h, step, by).start()
 
-    def add_core(h):
-        for j in range(3):
-            x_copy(j, h).wait_recv()
-
-            def one(x, _):
-                total = part[j, h, core, x].astype(F32) + from_core[j, h, x].astype(F32)
-                part[j, h, core, x] = total.astype(BF16)
-                return 0
-
-            lax.fori_loop(0, n, one, 0)
-            send(j, h, 0)
-
     def reduce(h, step):
         for j in range(3):
-            for by in range(1, n):
-                s_copy(j, h, step, by).wait_recv()
+            wait_for((recv1, recv2, recv3)[step].at[j, h], s_recv.at[step, j, h])
             total = own(j, h, step)
             for by in range(1, n):
                 total = total + (recv1, recv2, recv3)[step][j, h, by - 1].astype(F32)
@@ -234,55 +292,71 @@
                 (sum2, sum3)[step][j, h] = total.astype(BF16)
                 send(j, h, step + 1)
 
-    def grad_part(t, j):
-        at = slice(t * (labels // 2), (t + 1) * (labels // 2))
-        total = None
+    def grad_copy(t):
+        at = slice(t * (labels // 4), (t + 1) * (labels // 4))
+        return pltpu.make_async_copy(grad.at[at], grad_ref.at[at], grad_sem)
+
+    def grad_part(t):
+        size = labels // 4
+        at = slice(t * size, (t + 1) * size)
+        total = [None] * 3
         for h in range(2):
             for c in range(2):
-                d = delta[h, c, :, :, at].reshape(n * tile, labels // 2)
-                e = rows[j, c, :, :, :, half(h), :].reshape(n * tile, 256)
-                term = lax.dot_general(d, e, TN, preferred_element_type=F32)
-                total = term if total is None else total + term
-        grad_ref[at, j * 256 : (j + 1) * 256] = 0.5 * total
-
-    def block(h, c, send_it):
-        forward(h, c)
-        for j in range(3):
-            encoder_part(h, c, j)
-            if send_it:
-                x_copy(j, h).start()
-
-    block(0, other, True)
-    block(0, core, False)
-    add_core(0)
-    block(1, other, True)
+                d = delta[h, c, :, :, :, :, at].reshape(n * tile, size).T
+                for j in thirds:
+                    e = rows[j, c, :, :, :, half(h), :].reshape(n * tile, 256)
+                    term = jnp.dot(d, e, preferred_element_type=F32)
+                    total[j] = term if total[j] is None else total[j] + term
+        for j in thirds:
+            grad[at, j * 256 : (j + 1) * 256] = 0.5 * total[j]
+        grad_copy(t).start()
+
+    pass_on_ids()
+    for j in thirds:
+        g_start(j, 1, 1)
+    make_mask(core)
+    hand_on(0)
+    await_core((3,))
+    make_mask(other)
+    pass_on(0)
+    for j in thirds:
+        g_start(j, 2, 1)
+    forward(0, core)
+    await_core(thirds, 0)
+    forward(0, other)
+    hand_on(1)
+    for_sibling(0)
+    pass_on(1)
+    forward(1, core)
+    for_self(0)
+    await_core(thirds, 1)
+    forward(1, other)
+    for_sibling(1)
+    for_self(1)
     reduce(0, 0)
-    block(1, core, False)
-    add_core(1)
+    grad_part(0)
+    grad_part(1)
+    grad_part(2)
+    reduce(1, 0)
+    grad_part(3)
     reduce(0, 1)
-    grad_part(0, 0)
-    grad_part(0, 1)
+    reduce(1, 1)
     reduce(0, 2)
-    grad_part(0, 2)
-    reduce(1, 0)
-    grad_part(1, 0)
-    reduce(1, 1)
-    grad_part(1, 1)
     reduce(1, 2)
-    grad_part(1, 2)
-
-    for j in range(4):
-        for step in range(3):
-            for by in range(1, n):
-                g_copy(j, step, by).wait_send()
-        for by in range(n):
-            c_copy(j, by).wait_send()
-    for j in range(3):
-        for h in range(2):
-            x_copy(j, h).wait_send()
-            for step in range(3):
-                for by in range(1, n):
-                    s_copy(j, h, step, by).wait_send()
+
+    wait_for(grad, grad_sem)
+    whole = slice(None)
+    for step in range(3):
+        per = 2 if step == 2 and n == 4 else n - 1
+        index = (slice(0, per),) + ((0, 0), (whole, 0), (whole, whole))[step]
+        wait_for(rows.at[(whole, 0) + index], g_sent_all.at[step])
+        wait_for(ids.at[(0, slice(0, n - 1)) + index[1:]], id_sent.at[step])
+        wait_for((recv1, recv2, recv3)[step], s_sent.at[step])
+    if n == 4:
+        wait_for(rows.at[:, 0, 0], g_sent_half)
+    wait_for(rows.at[:, 0], c_sent.at[0])
+    wait_for(ids.at[0], c_sent.at[1])
+    wait_for(from_core, x_sent)
 
 
 def gradients(n, encoded, label_ids, weights):
@@ -298,11 +372,11 @@
         in_specs=[
             pl.BlockSpec(memory_space=pltpu.VMEM),
             pl.BlockSpec(memory_space=pltpu.VMEM),
-            pl.BlockSpec(memory_space=pl.ANY),
+            pl.BlockSpec(memory_space=pltpu.HBM),
         ],
         out_specs=(
             pl.BlockSpec(memory_space=pltpu.VMEM),
-            pl.BlockSpec(memory_space=pltpu.VMEM),
+            pl.BlockSpec(memory_space=pl.ANY),
         ),
         scratch_shapes=[
             vmem((3, 2, n, n, n, 32, 256), BF16),
@@ -310,7 +384,7 @@
             vmem((labels, width), F32),
             vmem((3, labels, 256), BF16),
             vmem((2 * n, n * n, 32, 128), jnp.int32),
-            vmem((2, 2, n, n * n * 16, labels), BF16),
+            vmem((2, 2, n, n, n, 16, labels), BF16),
             vmem((3, 2, 2, n, n, n, 16, 256), BF16),
             vmem((3, 2, n, n, n, 16, 256), BF16),
             vmem((3, 2, n - 1, n, n, 16, 256), BF16),
@@ -319,20 +393,25 @@
             vmem((3, 2, n, 16, 256), BF16),
             vmem((3, 2, n - 1, 16, 256), BF16),
             vmem((32, 128), jnp.int32),
+            vmem((labels, width), F32),
             dma,
-            dma((4, 3, n - 1)),
-            dma((4, 3, n - 1)),
-            dma((4, n)),
-            dma((4, n)),
+            dma,
+            dma((3,)),
+            dma,
+            dma((3,)),
+            dma((4, 2, 5)),
+            dma((2,)),
+            dma((4, 2)),
+            dma,
             dma((3, 2)),
-            dma((3, 2)),
-            dma((3, 3, 2, n - 1)),
-            dma((3, 3, 2, n - 1)),
+            dma((3,)),
+            dma((3, 3, 2)),
         ],
         compiler_params=pltpu.CompilerParams(
-            collective_id=0, has_side_effects=True, vmem_limit_bytes=60 * 2**20
+            collective_id=0, has_side_effects=True, vmem_limit_bytes=46 * 2**20
         ),
-    )(encoded, label_ids, weights)
+        name="gradients",
+    )(*(pltpu.with_memory_space_constraint(a, pltpu.HBM) for a in (encoded, label_ids, weights)))
 
 
 def on_device(n, encoded, label_ids, weights, accum):

time: 93.6 us -> 72.2 us (0.77); the launches traced: 93.5 us -> 70.9 us
  Pallas kernels: 86.1 us -> 64.4 us
    pallas_call x1, Pallas kernels: 86.1 us -> 64.4 us  [gradients(): pl.pallas_call(functools.partial(kernel, n), out_shape=(jax.ShapeDtypeStr...]
where the time goes in v2:
time: 72.2 us; the launch traced here: 70.9 us
  Pallas kernels  64.4 us (89%)
  other arithmetic  5.24 us (7%)
    pallas_call x1, Pallas kernels, gradients(): pl.pallas_call(functools.partial(kernel, n), out_shape=(jax.ShapeDtypeStr...  64.4 us
    sub x1, other arithmetic, on_device(): new_weights = weights - 0.5 * grad / jnp.sqrt(new_accum)  5.24 us

profile of v2, /device:TPU:0, one launch (start us, length us, event | category | flops | bytes accessed | tf_op | source)
XLA Modules:
  0.0 70.9 jit_solution(11926819905406272541)
XLA Ops:
  0.6 0.0 copy-start
  0.6 64.4 %gradients.1 = (bf16[32,768]{1,0:T(8,128)(2,1)S(1)}, f32[1024,768]{1,0:T(8,128)S(1)}) custom-call(bf16[32,768]{1,0:T(8,128)(2,1)} %enc_ref.1, s32[32,32]{1,0:T(8,128)} %ids_ref.1, f32[1024,768]{1,0:T(8,128)} %w_ref.1), custom_call_target="tpu_custom_call" | custom-call | tf_op jit(solution)/shard_map/gradients/pallas_call | solution.py:366
  65.1 0.0 copy-done
  65.1 5.2 %multiply_subtract_fusion = (f32[1024,768]{1,0:T(8,128)}, f32[1024,768]{1,0:T(8,128)}) fusion(f32[1024,768]{1,0:T(8,128)S(1)} %copy-done, f32[1024,768]{1,0:T(8,128)S(1)} %get-tuple-element.6, f32[1024,768]{1,0:T(8,128)} %param.7), kind=kLoop, calls=%fused_computation | loop fusion | flops 3932160 | bytes 15728640 | tf_op jit(solution)/shard_map/sub | solution.py:420
  70.3 0.6 copy.8
Async XLA Ops:
  0.6 64.4 %copy-start = (f32[1024,768]{1,0:T(8,128)S(1)}, f32[1024,768]{1,0:T(8,128)}, u32[]{:S(2)}) copy-start(f32[1024,768]{1,0:T(8,128)} %w_ref.1) | copy-start | bytes 9437188

commit v3 on v2

--- a/solution.py
+++ b/solution.py
@@ -10,7 +10,8 @@
 MESH = pl.DeviceIdType.MESH
 NT = (((1,), (1,)), ((), ()))
 TN = (((0,), (0,)), ((), ()))
-GATHER_ORDER = ((0, 1, 2), (1, 2, 0), (2, 0, 1), (0, 1, 2))
+GATHER_ORDER = ((0, 1, 2), (1, 2, 0), (2, 0, 1))
+ID_ORDER = ((0, 1, 2), (1, 2, 0))
 SCATTER_ORDER = ((0, 1, 2), (1, 2, 0), (2, 0, 1))
 F32 = jnp.float32
 BF16 = jnp.bfloat16
@@ -34,9 +35,9 @@
 
 
 def kernel(
-    n, enc_ref, ids_ref, w_ref, out_ref, grad_ref,
-    rows, ids, w_wide, w_low, mask, delta, part, from_core, recv1, sum2, recv2, sum3, recv3, pad, grad,
-    w_sem, grad_sem, g_sent_all, g_sent_half, id_sent, g_recv, c_sent, c_recv, x_sent, x_recv, s_sent, s_recv,
+    n, enc_ref, ids_ref, w_ref, a_ref, out_ref, new_w_ref, new_a_ref,
+    rows, ids, w_wide, w_low, mask, delta, part, from_core, recv1, sum2, recv2, sum3, recv3, pad, a_wide, held,
+    w_sem, a_sem, new_w_sem, new_a_sem, g_sent_all, g_sent_half, id_sent, g_recv, c_sent, c_recv, x_sent, x_recv, s_sent, s_recv,
 ):
     me, core = place(n)
     other = 1 - core
@@ -45,11 +46,14 @@
     offset = (batch * lax.axis_size("label") + label) * labels
     sibling = device(n, me, other)
 
+    far = (2, 1, 3) if n == 4 else tuple(range(n - 1, 0, -1))
+
     def shifted(axis, by):
         return tuple(lax.rem(me[a] + by, n) if a == axis else me[a] for a in range(3))
 
     w_copy = pltpu.make_async_copy(w_ref, w_wide, w_sem)
     w_copy.start()
+    pltpu.make_async_copy(a_ref, a_wide, a_sem).start()
 
     barrier = pltpu.get_barrier_semaphore()
     for axis in range(3):
@@ -89,42 +93,58 @@
     def block_of(j, index, h):
         return gathered(j, index + (half(h),) if j < 3 else index)
 
-    def g_sent(j, step):
-        return (id_sent if j == 3 else g_sent_all).at[step]
-
-    def g_copy(j, step, by, h=0, sem=None):
-        order = GATHER_ORDER[j]
+    def g_copy(j, step, by, h=0, sem=None, order=None):
+        order = order or GATHER_ORDER[j]
         index = tuple(slice(None) if a in order[:step] else me[a] for a in range(3))
         ref = block_of(j, index, h)
         to = device(n, shifted(order[step], by), core)
-        return remote(ref, ref, g_sent(j, step), g_recv.at[j, h, step if sem is None else sem], to)
+        sent = (id_sent if j == 3 else g_sent_all).at[step]
+        return remote(ref, ref, sent, g_recv.at[j, h, step if sem is None else sem], to)
 
     def g_wait(j, step, h=0):
-        order = GATHER_ORDER[j]
+        order = GATHER_ORDER[j % 3]
         index = tuple(
             slice(None) if a in order[:step] else slice(0, n - 1) if a == order[step] else 0 for a in range(3)
         )
         wait_for(block_of(j, index, h), g_recv.at[j, h, step])
 
+    def by_core(act):
+        for c in range(2):
+            pl.when(core == c)(functools.partial(act, ID_ORDER[c]))
+
+    def id_start(step):
+        if step > 0:
+            g_wait(3, step - 1)
+
+        def act(order):
+            if step == 2:
+                c_copy(3, 0, order=order).start()
+            for by in far:
+                g_copy(3, step, by, order=order).start()
+
+        by_core(act)
+
     def g_start(j, step, h=0):
+        if j == 3:
+            return id_start(step)
         if step > 0:
             g_wait(j, step - 1, h)
         if step == 2:
             c_copy(j, 0, h).start()
-        if step == 2 and j < 3 and n == 4:
+        if step == 2 and n == 4:
             g_copy(j, 2, 1, h, 2).start()
             g_copy(j, 2, 3, h, 3).start()
         else:
-            for by in range(1, n):
+            for by in far:
                 g_copy(j, step, by, h).start()
 
-    def plane(j, by, h, at=slice(None)):
-        first, _, last = GATHER_ORDER[j]
+    def plane(j, by, h, at=slice(None), order=None):
+        first, _, last = order or GATHER_ORDER[j]
         to = lax.rem(me[last] + n - by, n)
         return block_of(j, tuple(to if a == last else at if a == first else slice(None) for a in range(3)), h)
 
-    def c_copy(j, by, h=0):
-        ref = plane(j, by, h)
+    def c_copy(j, by, h=0, order=None):
+        ref = plane(j, by, h, order=order)
         return remote(ref, ref, c_sent.at[j // 3], c_recv.at[j, h], sibling)
 
     def hand_on(h):
@@ -149,8 +169,12 @@
 
     def pass_on_ids():
         g_wait(3, 2)
-        for by in range(1, n):
-            c_copy(3, by).start()
+
+        def act(order):
+            for by in range(1, n):
+                c_copy(3, by, order=order).start()
+
+        by_core(act)
 
     def await_core(js, h=0):
         for j in js:
@@ -203,8 +227,8 @@
             mask[cx, 4 * g : 4 * g + 4] = bits.reshape(4, 32, 128)
         return 0
 
-    def make_mask(c):
-        lax.fori_loop(c * n, c * n + n, mask_block, 0)
+    def make_mask(c, first, last):
+        lax.fori_loop(c * n + first, c * n + last, mask_block, 0)
 
     tile = n * n * 16
 
@@ -229,11 +253,17 @@
         r = jnp.dot(delta[h, c].reshape(n * tile, labels), w_low[j], preferred_element_type=F32)
         part[j, h, c] = (0.5 * r).astype(BF16).reshape(n, n, n, 16, 256)
 
-    def encoder_quarter(h, j, place):
-        at = tuple(place if a == j else slice(None) for a in range(3))
-        d = delta[(h, core) + at].reshape(tile, labels)
-        r = 0.5 * jnp.dot(d, w_low[j], preferred_element_type=F32)
-        r = r + from_core[(j, h) + at].reshape(tile, 256).astype(F32)
+    def quarter(j, by):
+        place = lax.rem(me[j] + by, n)
+        return tuple(place if a == j else slice(None) for a in range(3))
+
+    def quarter_sums(h, j, by):
+        d = delta[(h, core) + quarter(j, by)].reshape(tile, labels)
+        return 0.5 * jnp.dot(d, w_low[j], preferred_element_type=F32)
+
+    def add_sibling(h, j, by, sums):
+        at = quarter(j, by)
+        r = sums + from_core[(j, h) + at].reshape(tile, 256).astype(F32)
         part[(j, h, core) + at] = r.astype(BF16).reshape(n, n, 16, 256)
 
     def for_sibling(h):
@@ -244,18 +274,21 @@
         encoder_part(h, other, 2)
         x_copy(2, h).start()
 
-    def for_self(h):
+    def for_self(h, early):
+        order = far + (0,)
+        first = [(j, by) for by in order[: n // 2] for j in thirds]
+        rest = [(j, by) for by in order[n // 2 :] for j in thirds]
+        if early:
+            for i, (j, by) in enumerate(first):
+                held[i] = quarter_sums(h, j, by)
         for j in thirds:
             wait_for(from_core.at[j, h], x_recv.at[j, h])
-        far = (2, 1, 3, 0) if n == 4 else tuple(range(n - 1, -1, -1))
-        for some in (far[: n // 2], far[n // 2 :]):
-            for by in some:
-                for j in thirds:
-                    encoder_quarter(h, j, lax.rem(me[j] + by, n))
-            for by in some:
-                for j in thirds:
-                    if by > 0:
-                        s_copy(j, h, 0, by).start()
+        for some in (first, rest):
+            for i, (j, by) in enumerate(some):
+                add_sibling(h, j, by, held[i] if early and some is first else quarter_sums(h, j, by))
+            for j, by in some:
+                if by > 0:
+                    s_copy(j, h, 0, by).start()
 
     def x_copy(j, h):
         return remote(part.at[j, h, other], from_core.at[j, h], x_sent, x_recv.at[j, h], sibling)
@@ -277,7 +310,7 @@
         return ref[((j, h, core) if step == 0 else (j, h)) + index].astype(F32)
 
     def send(j, h, step):
-        for by in range(1, n):
+        for by in far:
             s_copy(j, h, step, by).start()
 
     def reduce(h, step):
@@ -291,10 +324,6 @@
             else:
                 (sum2, sum3)[step][j, h] = total.astype(BF16)
                 send(j, h, step + 1)
-
-    def grad_copy(t):
-        at = slice(t * (labels // 4), (t + 1) * (labels // 4))
-        return pltpu.make_async_copy(grad.at[at], grad_ref.at[at], grad_sem)
 
     def grad_part(t):
         size = labels // 4
@@ -308,32 +337,39 @@
                     term = jnp.dot(d, e, preferred_element_type=F32)
                     total[j] = term if total[j] is None else total[j] + term
         for j in thirds:
-            grad[at, j * 256 : (j + 1) * 256] = 0.5 * total[j]
-        grad_copy(t).start()
+            columns = slice(j * 256, (j + 1) * 256)
+            grad = 0.5 * total[j]
+            new = a_wide[at, columns] + grad * grad
+            a_wide[at, columns] = new
+            w_wide[at, columns] = w_wide[at, columns] - 0.5 * grad * lax.rsqrt(new)
+        pltpu.make_async_copy(a_wide.at[at], new_a_ref.at[at], new_a_sem).start()
+        pltpu.make_async_copy(w_wide.at[at], new_w_ref.at[at], new_w_sem).start()
 
     pass_on_ids()
     for j in thirds:
         g_start(j, 1, 1)
-    make_mask(core)
+    make_mask(core, 0, n)
     hand_on(0)
     await_core((3,))
-    make_mask(other)
-    pass_on(0)
+    make_mask(other, 0, n // 2)
     for j in thirds:
         g_start(j, 2, 1)
+    make_mask(other, n // 2, n)
+    pass_on(0)
     forward(0, core)
+    hand_on(1)
     await_core(thirds, 0)
     forward(0, other)
-    hand_on(1)
     for_sibling(0)
     pass_on(1)
     forward(1, core)
-    for_self(0)
+    for_self(0, False)
     await_core(thirds, 1)
     forward(1, other)
     for_sibling(1)
-    for_self(1)
+    for_self(1, True)
     reduce(0, 0)
+    wait_for(a_wide, a_sem)
     grad_part(0)
     grad_part(1)
     grad_part(2)
@@ -344,7 +380,8 @@
     reduce(0, 2)
     reduce(1, 2)
 
-    wait_for(grad, grad_sem)
+    wait_for(a_wide, new_a_sem)
+    wait_for(w_wide, new_w_sem)
     whole = slice(None)
     for step in range(3):
         per = 2 if step == 2 and n == 4 else n - 1
@@ -359,23 +396,26 @@
     wait_for(from_core, x_sent)
 
 
-def gradients(n, encoded, label_ids, weights):
+def step(n, encoded, label_ids, weights, accum):
     labels, width = weights.shape
     vmem = pltpu.VMEM
     dma = pltpu.SemaphoreType.DMA
-    return pl.pallas_call(
+    results = pl.pallas_call(
         functools.partial(kernel, n),
         out_shape=(
             jax.ShapeDtypeStruct(encoded.shape, BF16),
+            jax.ShapeDtypeStruct((labels, width), F32),
             jax.ShapeDtypeStruct((labels, width), F32),
         ),
         in_specs=[
             pl.BlockSpec(memory_space=pltpu.VMEM),
             pl.BlockSpec(memory_space=pltpu.VMEM),
             pl.BlockSpec(memory_space=pltpu.HBM),
+            pl.BlockSpec(memory_space=pltpu.HBM),
         ],
         out_specs=(
             pl.BlockSpec(memory_space=pltpu.VMEM),
+            pl.BlockSpec(memory_space=pl.ANY),
             pl.BlockSpec(memory_space=pl.ANY),
         ),
         scratch_shapes=[
@@ -394,6 +434,9 @@
             vmem((3, 2, n - 1, 16, 256), BF16),
             vmem((32, 128), jnp.int32),
             vmem((labels, width), F32),
+            vmem((3 * (n // 2), n * n * 16, 256), F32),
+            dma,
+            dma,
             dma,
             dma,
             dma((3,)),
@@ -411,21 +454,43 @@
             collective_id=0, has_side_effects=True, vmem_limit_bytes=46 * 2**20
         ),
         name="gradients",
-    )(*(pltpu.with_memory_space_constraint(a, pltpu.HBM) for a in (encoded, label_ids, weights)))
-
-
-def on_device(n, encoded, label_ids, weights, accum):
-    encoder_grad, grad = gradients(n, encoded, label_ids, weights)
-    new_accum = accum + grad * grad
-    new_weights = weights - 0.5 * grad / jnp.sqrt(new_accum)
-    return (encoder_grad, new_weights, new_accum)
+    )(*(pltpu.with_memory_space_constraint(a, pltpu.HBM) for a in (encoded, label_ids, weights, accum)))
+    return store(*results)
+
+
+def store_kernel(pieces, *refs):
+    count = len(pieces)
+    sources, targets, sems = refs[:count], refs[count : 2 * count], refs[2 * count]
+    copies = []
+    for source, target, parts in zip(sources, targets, pieces):
+        size = source.shape[0] // parts
+        for p in range(parts):
+            at = pl.ds(p * size, size)
+            copies.append(pltpu.make_async_copy(source.at[at], target.at[at], sems.at[len(copies)]))
+    for copy in copies:
+        copy.start()
+    for copy in copies:
+        copy.wait()
+
+
+def store(*arrays):
+    pieces = (1, 4, 4)
+    return pl.pallas_call(
+        functools.partial(store_kernel, pieces),
+        out_shape=tuple(jax.ShapeDtypeStruct(a.shape, a.dtype) for a in arrays),
+        in_specs=[pl.BlockSpec(memory_space=pltpu.VMEM)] * len(arrays),
+        out_specs=(pl.BlockSpec(memory_space=pltpu.HBM),) * len(arrays),
+        scratch_shapes=[pltpu.SemaphoreType.DMA((sum(pieces),))],
+        compiler_params=pltpu.CompilerParams(vmem_limit_bytes=16 * 2**20),
+        name="store",
+    )(*arrays)
 
 
 def solution(mesh):
     n = {4: 2, 32: 4}[mesh.shape["label"]]
     rows = P(("batch", "label"), None)
     return jax.shard_map(
-        functools.partial(on_device, n),
+        functools.partial(step, n),
         mesh=mesh,
         in_specs=(rows, rows, rows, rows),
         out_specs=(rows, rows, rows),

time: 72.2 us -> 65.7 us (0.910); the launches traced: 70.9 us -> 65.2 us
  other arithmetic: 5.24 us -> 0 us
    sub x1 -> x0, other arithmetic: 5.24 us -> none  [on_device(): new_weights = weights - 0.5 * grad / jnp.sqrt(new_accum)]
    pallas_call x1 -> x2, Pallas kernels: 64.4 us -> 64.3 us  [the longest x1 61.6 us: step(): pl.pallas_call(functools.partial(kernel, n), out_shape=(jax.ShapeDtypeStr...]
where the time goes in v3:
time: 65.7 us; the launch traced here: 65.2 us
  Pallas kernels  64.3 us (98%)
  between operations  0.82 us (1%)
    pallas_call x1, Pallas kernels, step(): pl.pallas_call(functools.partial(kernel, n), out_shape=(jax.ShapeDtypeStr...  61.6 us
    pallas_call x1, Pallas kernels, store(): pl.pallas_call(functools.partial(store_kernel, pieces), out_shape=tuple((...  2.77 us

profile of v3, /device:TPU:0, one launch (start us, length us, event | category | flops | bytes accessed | tf_op | source)
XLA Modules:
  0.0 65.2 jit_solution(17054234086892561008)
XLA Ops:
  0.6 61.6 %gradients.1 = (bf16[32,768]{1,0:T(8,128)(2,1)S(1)}, f32[1024,768]{1,0:T(8,128)S(1)}, f32[1024,768]{1,0:T(8,128)S(1)}) custom-call(bf16[32,768]{1,0:T(8,128)(2,1)} %enc_ref.1, s32[32,32]{1,0:T(8,128)} %ids_ref.1, f32[1024,768]{1,0:T(8,128)} %w_ref.1, f32[1024,768]{1,0:T(8,128)} %a_ref.1), custom_call_target="tpu_custom_call" | custom-call | tf_op jit(solution)/shard_map/gradients/pallas_call | solution.py:403
  62.2 2.8 %store.1 = (bf16[32,768]{1,0:T(8,128)(2,1)}, f32[1024,768]{1,0:T(8,128)}, f32[1024,768]{1,0:T(8,128)}) custom-call(bf16[32,768]{1,0:T(8,128)(2,1)S(1)} %get-tuple-element.6.refs_0_, f32[1024,768]{1,0:T(8,128)S(1)} %get-tuple-element.7.refs_1_, f32[1024,768]{1,0:T(8,128)S(1)} %get-tuple-element.8.refs_2_), custom_call_target="tpu_custom_call" | custom-call | tf_op jit(solution)/shard_map/store/pallas_call | solution.py:478

commit v4 on v3

--- a/solution.py
+++ b/solution.py
@@ -37,7 +37,7 @@
 def kernel(
     n, enc_ref, ids_ref, w_ref, a_ref, out_ref, new_w_ref, new_a_ref,
     rows, ids, w_wide, w_low, mask, delta, part, from_core, recv1, sum2, recv2, sum3, recv3, pad, a_wide, held,
-    w_sem, a_sem, new_w_sem, new_a_sem, g_sent_all, g_sent_half, id_sent, g_recv, c_sent, c_recv, x_sent, x_recv, s_sent, s_recv,
+    w_sem, a_sem, new_w_sem, new_a_sem, g_sent_all, g_sent_half, id_sent, g_recv, c_sent, c_recv, x_sent, x_recv, s_sent, s_recv, s_relay,
 ):
     me, core = place(n)
     other = 1 - core
@@ -287,7 +287,9 @@
             for i, (j, by) in enumerate(some):
                 add_sibling(h, j, by, held[i] if early and some is first else quarter_sums(h, j, by))
             for j, by in some:
-                if by > 0:
+                if by > 0 and early and n == 4:
+                    by_halves(j, by)
+                elif by > 0:
                     s_copy(j, h, 0, by).start()
 
     def x_copy(j, h):
@@ -302,6 +304,34 @@
         dst = (recv1, recv2, recv3)[step].at[j, h, by - 1]
         return remote(src, dst, s_sent.at[step], s_recv.at[step, j, h], device(n, to, core))
 
+    def half_block(j, by, upper):
+        cut = slice(n // 2, n) if upper else slice(0, n // 2)
+        place = lax.rem(me[j] + by, n)
+        other_axis = 1 if j == 0 else 0
+        index = tuple(place if a == j else cut if a == other_axis else slice(None) for a in range(3))
+        return (j, 1, core) + index, cut
+
+    def half_copy(j, by, upper, to, slot, sem):
+        at, cut = half_block(j, by, upper)
+        return remote(part.at[at], recv1.at[j, 1, slot, cut], s_sent.at[0], sem, device(n, shifted(j, to), core))
+
+    def by_halves(j, by):
+        if by == 2:
+            half_copy(j, 2, False, 1, 1, s_relay.at[j]).start()
+            half_copy(j, 2, True, 3, 1, s_relay.at[j]).start()
+        else:
+            half_copy(j, by, by == 1, by, by - 1, s_recv.at[0, j, 1]).start()
+
+    def relay():
+        if n == 4:
+            for j in thirds:
+                wait_for(recv1.at[j, 1, 1], s_relay.at[j])
+                for by in (1, 3):
+                    at, cut = half_block(j, by, by == 3)
+                    part[at] = (part[at].astype(F32) + recv1[j, 1, 1, cut].astype(F32)).astype(BF16)
+                for by in (1, 3):
+                    half_copy(j, by, by == 3, by, by - 1, s_recv.at[0, j, 1]).start()
+
     def own(j, h, step):
         order = SCATTER_ORDER[j]
         left = [a for a in range(3) if a not in order[:step]]
@@ -315,9 +345,11 @@
 
     def reduce(h, step):
         for j in range(3):
-            wait_for((recv1, recv2, recv3)[step].at[j, h], s_recv.at[step, j, h])
+            halved = n == 4 and h == 1 and step == 0
+            arrived = (recv1, recv2, recv3)[step].at[j, h]
+            wait_for(arrived.at[0:2] if halved else arrived, s_recv.at[step, j, h])
             total = own(j, h, step)
-            for by in range(1, n):
+            for by in (1, 3) if halved else range(1, n):
                 total = total + (recv1, recv2, recv3)[step][j, h, by - 1].astype(F32)
             if step == 2:
                 out_ref[half(h), j * 256 : (j + 1) * 256] = total.astype(BF16)
@@ -368,15 +400,16 @@
     forward(1, other)
     for_sibling(1)
     for_self(1, True)
-    reduce(0, 0)
     wait_for(a_wide, a_sem)
     grad_part(0)
+    relay()
+    reduce(0, 0)
     grad_part(1)
+    reduce(1, 0)
     grad_part(2)
-    reduce(1, 0)
-    grad_part(3)
     reduce(0, 1)
     reduce(1, 1)
+    grad_part(3)
     reduce(0, 2)
     reduce(1, 2)
 
@@ -449,6 +482,7 @@
             dma((3, 2)),
             dma((3,)),
             dma((3, 3, 2)),
+            dma((3,)),
         ],
         compiler_params=pltpu.CompilerParams(
             collective_id=0, has_side_effects=True, vmem_limit_bytes=46 * 2**20

time: 65.7 us -> 65.4 us (level)
  no operation moved by 1% of the time
where the time goes in v4:
time: 65.4 us; the launch traced here: 65.3 us
  Pallas kernels  64.4 us (98%)
  between operations  0.82 us (1%)
    pallas_call x1, Pallas kernels, step(): pl.pallas_call(functools.partial(kernel, n), out_shape=(jax.ShapeDtypeStr...  61.7 us
    pallas_call x1, Pallas kernels, store(): pl.pallas_call(functools.partial(store_kernel, pieces), out_shape=tuple((...  2.77 us

profile of v4, /device:TPU:0, one launch (start us, length us, event | category | flops | bytes accessed | tf_op | source)
XLA Modules:
  0.0 65.3 jit_solution(9183228201586973545)
XLA Ops:
  0.6 61.7 %gradients.1 = (bf16[32,768]{1,0:T(8,128)(2,1)S(1)}, f32[1024,768]{1,0:T(8,128)S(1)}, f32[1024,768]{1,0:T(8,128)S(1)}) custom-call(bf16[32,768]{1,0:T(8,128)(2,1)} %enc_ref.1, s32[32,32]{1,0:T(8,128)} %ids_ref.1, f32[1024,768]{1,0:T(8,128)} %w_ref.1, f32[1024,768]{1,0:T(8,128)} %a_ref.1), custom_call_target="tpu_custom_call" | custom-call | tf_op jit(solution)/shard_map/gradients/pallas_call | solution.py:436
  62.3 2.8 %store.1 = (bf16[32,768]{1,0:T(8,128)(2,1)}, f32[1024,768]{1,0:T(8,128)}, f32[1024,768]{1,0:T(8,128)}) custom-call(bf16[32,768]{1,0:T(8,128)(2,1)S(1)} %get-tuple-element.6.refs_0_, f32[1024,768]{1,0:T(8,128)S(1)} %get-tuple-element.7.refs_1_, f32[1024,768]{1,0:T(8,128)S(1)} %get-tuple-element.8.refs_2_), custom_call_target="tpu_custom_call" | custom-call | tf_op jit(solution)/shard_map/store/pallas_call | solution.py:512
